TPU v7x, 128 devices: a whole 4x4x4 slice. The times are simulated.
128 devices in a mesh: dp: 16 (over y_lo, z, core), ctx: 8 (over y_hi, x).
Axes of the slice: x: 4, y: 4 (y_hi: 2, y_lo: 2; y = y_hi * 2 + y_lo), z: 4, core: 2. Of those that a mesh axis runs over, the one named last changes fastest.
Arguments:
- inputs: bfloat16 [32, 1024, 1024], P('dp', 'ctx'), may hold values from -6 to 6
- positions: int32 [32, 1024], P('dp'), may hold values from 0 to 1023, as said below
- first_gain: float32 [1024], replicated, may hold values from 0.5 to 1.5
- first_shift: float32 [1024], replicated, may hold values from -4 to 4
- second_gain: float32 [1024], replicated, may hold values from 0.5 to 1.5
- second_shift: float32 [1024], replicated, may hold values from -4 to 4
- project_weight: bfloat16 [1024, 3072], P(('dp', 'ctx')), may hold values from -0.1875 to 0.1875
- project_bias: float32 [3072], replicated, may hold values from -4 to 4
- output_weight: bfloat16 [1024, 1024], P(('dp', 'ctx')), may hold values from -2 to 2
- output_bias: float32 [1024], replicated, may hold values from -4 to 4
- expand_weight: bfloat16 [1024, 4096], P(('dp', 'ctx')), may hold values from -0.1875 to 0.1875
- expand_bias: float32 [4096], replicated, may hold values from -4 to 4
- reduce_weight: bfloat16 [1024, 4, 1024], P(('dp', 'ctx')), may hold values from -0.09375 to 0.09375
- reduce_bias: float32 [1024], replicated, may hold values from -4 to 4
- cotangent: bfloat16 [32, 1024, 1024], P('dp', 'ctx'), may hold values from -6 to 6
Outputs:
- block_output: bfloat16 [32, 1024, 1024], P('dp', 'ctx')
- inputs_grad: bfloat16 [32, 1024, 1024], P('dp', 'ctx')
- first_gain_grad: float32 [1024], P(('dp', 'ctx'))
- first_shift_grad: float32 [1024], P(('dp', 'ctx'))
- second_gain_grad: float32 [1024], P(('dp', 'ctx'))
- second_shift_grad: float32 [1024], P(('dp', 'ctx'))
- project_weight_grad: float32 [1024, 3072], P(('dp', 'ctx'))
- project_bias_grad: float32 [3072], P(('dp', 'ctx'))
- output_weight_grad: float32 [1024, 1024], P(('dp', 'ctx'))
- output_bias_grad: float32 [1024], P(('dp', 'ctx'))
- expand_weight_grad: float32 [1024, 4096], P(('dp', 'ctx'))
- expand_bias_grad: float32 [4096], P(('dp', 'ctx'))
- reduce_weight_grad: float32 [1024, 4, 1024], P(('dp', 'ctx'))
- reduce_bias_grad: float32 [1024], P(('dp', 'ctx'))
Inputs may be any that keep to these rules, and one draw needn't show every extreme that they name: Each row is a permutation of the positions of a sequence. The 128 stored rows of ctx index c (rows c * 128 onward) are the positions p * 64 to (p + 1) * 64 - 1 in order, then (15 - p) * 64 to (16 - p) * 64 - 1 in order, where p runs over a permutation of the ctx indices drawn for each sequence.
All inputs are finite; a program needn't handle non-finite values.
Results may differ from a plain program's by a relative error of at most 0.014.
Values may be sent and summed in bfloat16 or wider, within the bound.
A program may use at most 320 MiB of HBM per device.

v0:
```python
import jax
import jax.numpy as jnp
from jax import lax
from jax.sharding import PartitionSpec as P

D = 1024
HEADS = 16
HD = 64
ROT = 16
FF = 4096
GROUPS = 4


EPSILON = 1e-05


def side_by_side(arrays, axis, dim, along):
    both = jnp.concatenate(arrays, axis=along)
    whole, at, done = (lax.psum_scatter(both, axis, scatter_dimension=dim, tiled=True), 0, [])
    for a in arrays:
        done.append(lax.slice_in_dim(whole, at, at + a.shape[along], axis=along))
        at += a.shape[along]
    return tuple(done)


def rotary_tables(places):
    halfway = ROT // 2
    inverse = 10000.0 ** (-(jnp.arange(halfway, dtype=jnp.float32) * 2.0 / ROT))
    turned = places.astype(jnp.float32)[..., None] * inverse
    return (jnp.cos(turned)[..., None, :], jnp.sin(turned)[..., None, :])


def rotate(tensor, cosine, sine):
    halfway = ROT // 2
    leading = tensor[..., :halfway]
    trailing = tensor[..., halfway:ROT]
    return jnp.concatenate(
        [leading * cosine - trailing * sine, trailing * cosine + leading * sine, tensor[..., ROT:]],
        axis=-1,
    )


def across(left, right):
    return lax.dot_general(
        left, right, (((1,), (1,)), ((), ())), preferred_element_type=jnp.float32
    )


def down_rows(left, right):
    return lax.dot_general(
        left, right, (((0,), (0,)), ((), ())), preferred_element_type=jnp.float32
    )


def make_terms(kept, count):
    first_all, second_all, attended_all, hidden_all, d_project_all, d_expand_all, upstream_all = (
        kept
    )
    hidden_all_groups = hidden_all.reshape(hidden_all.shape[0], GROUPS, D)
    term_project = down_rows(first_all, d_project_all)
    term_expand = down_rows(second_all, d_expand_all)
    term_output = down_rows(attended_all, upstream_all)
    term_reduce = jnp.einsum(
        "rkn,re->nke", hidden_all_groups, upstream_all, preferred_element_type=jnp.float32
    ).reshape(count, GROUPS * D)
    return jnp.concatenate([term_project, term_expand, term_output, term_reduce], axis=1)


def shards(
    inputs,
    positions,
    first_gain,
    first_shift,
    second_gain,
    second_shift,
    project_weight,
    project_bias,
    output_weight,
    output_bias,
    expand_weight,
    expand_bias,
    reduce_weight,
    reduce_bias,
    cotangent,
):
    seq_count = inputs.shape[0]
    local_len = inputs.shape[1]
    full_len = positions.shape[1]
    ctx_index = lax.axis_index("ctx")
    scaling = HD ** (-0.5)

    def process(opening, closing):
        batch = closing - opening
        total_rows = batch * local_len
        widened = inputs.astype(jnp.float32).reshape(total_rows, D)
        centred = widened - jnp.mean(widened, axis=-1, keepdims=True)
        inv_scale = lax.rsqrt(jnp.mean(centred * centred, axis=-1, keepdims=True) + EPSILON)
        normed = centred * inv_scale
        first_in = (normed * first_gain + first_shift).astype(jnp.bfloat16)
        second_in = (normed * second_gain + second_shift).astype(jnp.bfloat16)
        pieces = (
            lax.all_gather(project_weight, ("dp", "ctx"), axis=0, tiled=True),
            lax.all_gather(expand_weight, ("dp", "ctx"), axis=0, tiled=True),
        )
        pre_project = jnp.dot(first_in, pieces[0], preferred_element_type=jnp.float32)
        pre_expand = jnp.dot(second_in, pieces[1], preferred_element_type=jnp.float32)
        projected = pre_project + project_bias
        local_places = lax.dynamic_slice_in_dim(positions, ctx_index * local_len, local_len, 1)
        cosine, sine = rotary_tables(local_places)
        queries = rotate(
            projected[:, :D].reshape(batch, local_len, HEADS, HD), cosine, sine
        ).astype(jnp.bfloat16)
        keys_local = rotate(
            projected[:, D : 2 * D].reshape(batch, local_len, HEADS, HD), cosine, sine
        ).astype(jnp.bfloat16)
        values_local = projected[:, 2 * D :].reshape(batch, local_len, D).astype(jnp.bfloat16)
        keys_all, values_all = (
            lax.all_gather(keys_local.reshape(batch, local_len, D), "ctx", axis=1, tiled=True),
            lax.all_gather(values_local, "ctx", axis=1, tiled=True),
        )
        key_heads = keys_all.reshape(batch, full_len, HEADS, HD)
        value_heads = values_all.reshape(batch, full_len, HEADS, HD)
        allowed = positions[:, None, None, :] <= local_places[:, None, :, None]
        scores = (
            jnp.einsum("mqhd,mkhd->mhqk", queries, key_heads, preferred_element_type=jnp.float32)
            * scaling
        )
        scores = jnp.where(allowed, scores, -1e30)
        highest = jnp.max(scores, axis=-1, keepdims=True)
        raised = jnp.exp(scores - highest)
        denominator = jnp.sum(raised, axis=-1, keepdims=True)
        log_total = highest + jnp.log(denominator)
        probs_low = (raised / denominator).astype(jnp.bfloat16)
        attended = jnp.einsum(
            "mhqk,mkhd->mqhd", probs_low, value_heads, preferred_element_type=jnp.float32
        )
        attended_low = attended.reshape(total_rows, D).astype(jnp.bfloat16)
        expanded = pre_expand + expand_bias
        hidden_low = jax.nn.gelu(expanded, approximate=False).astype(jnp.bfloat16)
        hidden_groups = hidden_low.reshape(total_rows, GROUPS, D)
        pieces = (
            lax.all_gather(output_weight, ("dp", "ctx"), axis=0, tiled=True),
            lax.all_gather(reduce_weight, ("dp", "ctx"), axis=0, tiled=True),
        )
        running = jnp.dot(attended_low, pieces[0], preferred_element_type=jnp.float32)
        branches = running + jnp.einsum(
            "rkn,nke->re", hidden_groups, pieces[1], preferred_element_type=jnp.float32
        )
        block_out = (
            (widened + branches + output_bias + reduce_bias)
            .astype(jnp.bfloat16)
            .reshape(batch, local_len, D)
        )
        upstream = cotangent.reshape(total_rows, D)
        upstream_wide = upstream.astype(jnp.float32)
        pieces = lax.all_gather((output_weight, reduce_weight), ("dp", "ctx"), axis=0, tiled=True)
        back_att = across(upstream, pieces[0])
        back_hid = jnp.einsum(
            "re,nke->rkn", upstream, pieces[1], preferred_element_type=jnp.float32
        )
        second_result = jnp.concatenate([back_att[:, None, :], back_hid], axis=1)
        d_attended = second_result[:, 0, :]
        d_hidden = second_result[:, 1:, :].reshape(total_rows, FF)
        unused, gelu_back = jax.vjp(
            lambda pre_act: jax.nn.gelu(pre_act, approximate=False), expanded
        )
        d_expanded = gelu_back(d_hidden)[0]
        d_expanded_low = d_expanded.astype(jnp.bfloat16)
        d_out = d_attended.astype(jnp.bfloat16).reshape(batch, local_len, HEADS, HD)
        again = (
            jnp.einsum("mqhd,mkhd->mhqk", queries, key_heads, preferred_element_type=jnp.float32)
            * scaling
        )
        again = jnp.where(allowed, again, -1e30)
        probs_again = jnp.exp(again - log_total)
        d_probs = jnp.einsum(
            "mqhd,mkhd->mhqk", d_out, value_heads, preferred_element_type=jnp.float32
        )
        row_delta = jnp.sum(d_probs * probs_again, axis=-1, keepdims=True)
        d_scores = (probs_again * (d_probs - row_delta)).astype(jnp.bfloat16)
        d_queries = (
            jnp.einsum("mhqk,mkhd->mqhd", d_scores, key_heads, preferred_element_type=jnp.float32)
            * scaling
        )
        key_terms = (
            jnp.einsum("mhqk,mqhd->mkhd", d_scores, queries, preferred_element_type=jnp.float32)
            * scaling
        ).reshape(batch, full_len, D)
        value_terms = jnp.einsum(
            "mhqk,mqhd->mkhd",
            probs_again.astype(jnp.bfloat16),
            d_out,
            preferred_element_type=jnp.float32,
        ).reshape(batch, full_len, D)
        d_keys, d_values = tuple(
            (
                part.astype(jnp.float32)
                for part in side_by_side(
                    (key_terms.astype(jnp.bfloat16), value_terms.astype(jnp.bfloat16)), "ctx", 1, 0
                )
            )
        )
        query_back = rotate(d_queries, cosine, -sine).reshape(total_rows, D)
        key_back = rotate(d_keys.reshape(batch, local_len, HEADS, HD), cosine, -sine).reshape(
            total_rows, D
        )
        d_projected = jnp.concatenate(
            [query_back, key_back, d_values.reshape(total_rows, D)], axis=1
        )
        d_projected_low = d_projected.astype(jnp.bfloat16)
        pieces = lax.all_gather((project_weight, expand_weight), ("dp", "ctx"), axis=0, tiled=True)
        first_result = jnp.stack(
            [across(d_projected_low, pieces[0]), across(d_expanded_low, pieces[1])], axis=1
        )
        d_first = first_result[:, 0, :]
        d_second = first_result[:, 1, :]
        small_terms = (
            jnp.sum(d_first * normed, axis=0),
            jnp.sum(d_first, axis=0),
            jnp.sum(d_second * normed, axis=0),
            jnp.sum(d_second, axis=0),
            jnp.sum(d_projected, axis=0),
            jnp.sum(upstream_wide, axis=0),
            jnp.sum(d_expanded, axis=0),
        )
        d_normed = d_first * first_gain + d_second * second_gain
        d_inputs = upstream_wide + inv_scale * (
            d_normed
            - jnp.mean(d_normed, axis=-1, keepdims=True)
            - normed * jnp.mean(d_normed * normed, axis=-1, keepdims=True)
        )
        kept = (
            first_in,
            second_in,
            attended_low,
            hidden_low,
            d_projected_low,
            d_expanded_low,
            upstream,
        )
        return (
            block_out,
            d_inputs.astype(jnp.bfloat16).reshape(batch, local_len, D),
            small_terms,
            kept,
        )

    own_rows = project_weight.shape[0]
    spans = (0, seq_count)
    opening, closing = spans
    entry = process(opening, closing)
    results = [entry]
    shares = lax.psum_scatter(
        make_terms(entry[3], lax.axis_size(("dp", "ctx")) * own_rows),
        ("dp", "ctx"),
        scatter_dimension=0,
        tiled=True,
    )
    block_output = jnp.concatenate([entry[0] for entry in results], axis=0)
    inputs_grad = jnp.concatenate([entry[1] for entry in results], axis=0)
    small_sums = results[0][2]
    project_weight_grad = shares[:, : 3 * D]
    expand_weight_grad = shares[:, 3 * D : 3 * D + FF]
    output_weight_grad = shares[:, 3 * D + FF : 4 * D + FF]
    reduce_weight_grad = shares[:, 4 * D + FF :].reshape(own_rows, GROUPS, D)
    small_out = lax.psum_scatter(small_sums, ("dp", "ctx"), scatter_dimension=0, tiled=True)
    return (
        block_output,
        inputs_grad,
        small_out[0],
        small_out[1],
        small_out[2],
        small_out[3],
        project_weight_grad,
        small_out[4],
        output_weight_grad,
        small_out[5],
        expand_weight_grad,
        small_out[6],
        reduce_weight_grad,
        small_out[5],
    )


def solution(mesh):
    return jax.shard_map(
        shards,
        mesh=mesh,
        in_specs=(
            P("dp", "ctx", None),
            P("dp", None),
            P(),
            P(),
            P(),
            P(),
            P(("dp", "ctx"), None),
            P(),
            P(("dp", "ctx"), None),
            P(),
            P(("dp", "ctx"), None),
            P(),
            P(("dp", "ctx"), None, None),
            P(),
            P("dp", "ctx", None),
        ),
        out_specs=(
            P("dp", "ctx", None),
            P("dp", "ctx", None),
            P(("dp", "ctx")),
            P(("dp", "ctx")),
            P(("dp", "ctx")),
            P(("dp", "ctx")),
            P(("dp", "ctx"), None),
            P(("dp", "ctx")),
            P(("dp", "ctx"), None),
            P(("dp", "ctx")),
            P(("dp", "ctx"), None),
            P(("dp", "ctx")),
            P(("dp", "ctx"), None, None),
            P(("dp", "ctx")),
        ),
        check_vma=False,
    )
```

profile of v0, /device:TPU:0, one launch (start us, length us, event | category | flops | bytes accessed | tf_op | source)
XLA Modules:
  0.0 2364.7 jit_solution(1085330817322379191)
XLA Ops:
  8.7 1.3 fusion.56
  10.0 1.2 convert_reduce_fusion.1
  11.2 1.3 multiply_reduce_fusion.4
  13.3 2.2 add_convert_fusion.2
  15.5 307.3 %all-gather.7.cloned.1.call-done = bf16[1024,3072]{1,0:T(8,128)(2,1)} async-done(((bf16[8,3072]{1,0:T(8,128)(2,1)}), bf16[1024,3072]{1,0:T(8,128)(2,1)}) %all-gather.7.cloned.1.call-update) | async-done | bytes 6291472 | tf_op jit(solution)/shard_map/all_gather | solution.py:102
  322.8 4.6 convolution_add_fusion.1
  327.6 1.5 copy-done.20
  331.6 2.6 fusion.58
  334.2 2.3 copy.118
  336.5 2.4 copy.117
  338.9 1.0 fusion.59
  342.4 2.1 slice.119
  344.6 1.5 copy.89
  347.7 278.9 %all-gather.13.cloned.1.call-done = bf16[1024,1024]{1,0:T(8,128)(2,1)} async-done(((bf16[8,1024]{1,0:T(8,128)(2,1)}), bf16[1024,1024]{1,0:T(8,128)(2,1)}) %all-gather.13.cloned.1.call-update) | async-done | bytes 2097168 | tf_op jit(solution)/shard_map/all_gather | solution.py:142
  626.5 2.3 convolution_convert_fusion
  628.9 1.6 reshape.204
  630.5 2.0 copy.92
  632.5 1.3 slice.91
  633.8 2.0 copy.119
  635.8 72.5 %all-gather.11.cloned.1.call-done = bf16[2,1024,1024]{1,2,0:T(8,128)(2,1)} async-done(((bf16[2,128,1024]{1,2,0:T(8,128)(2,1)}), bf16[2,1024,1024]{1,2,0:T(8,128)(2,1)}) %all-gather.11.cloned.1.call-update) | async-done | bytes 4194320 | tf_op jit(solution)/shard_map/all_gather | solution.py:118
  708.3 5.3 fusion.61
  713.7 3.8 fusion
  717.5 1.9 copy-done
  719.4 9.1 fusion.12
  728.6 6.2 copy.96
  734.8 46.6 %all-gather.9.cloned.1.call-done = bf16[2,1024,1024]{2,1,0:T(8,128)(2,1)} async-done(((bf16[2,128,1024]{2,1,0:T(8,128)(2,1)}), bf16[2,1024,1024]{2,1,0:T(8,128)(2,1)}) %all-gather.9.cloned.1.call-update) | async-done | bytes 4194320 | tf_op jit(solution)/shard_map/all_gather | solution.py:119
  781.5 6.2 copy.77
  787.7 12.3 multiply_reduce_fusion
  800.0 11.9 multiply_convert_fusion
  811.9 3.8 multiply_convert_fusion.1
  816.4 6.2 copy.95
  822.6 7.5 pad_maximum_fusion.1
  830.2 263.1 %all-gather.17.cloned.1.call-done = bf16[1024,4,1024]{2,0,1:T(8,128)(2,1)} async-done(((bf16[8,4,1024]{2,0,1:T(8,128)(2,1)}), bf16[1024,4,1024]{2,0,1:T(8,128)(2,1)}) %all-gather.17.cloned.1.call-update) | async-done | bytes 8388624 | tf_op jit(solution)/shard_map/all_gather | solution.py:143
  1093.2 7.8 fusion.62
  1101.0 5.8 copy.108
  1106.8 300.4 %all-gather.15.cloned.1.call-done = bf16[1024,4096]{1,0:T(8,128)(2,1)} async-done(((bf16[8,4096]{1,0:T(8,128)(2,1)}), bf16[1024,4096]{1,0:T(8,128)(2,1)}) %all-gather.15.cloned.1.call-update) | async-done | bytes 8388624 | tf_op jit(solution)/shard_map/all_gather | solution.py:103
  1407.3 15.9 fusion.54
  1423.9 8.7 fusion.17
  1432.5 17.7 copy.110
  1450.2 10.1 fusion.34
  1460.3 8.5 fusion.32
  1469.4 3.0 fusion.26
  1474.4 2.7 fusion.38
  1477.0 49.9 %reduce-scatter.3.cloned.1.call-done = bf16[4,128,1024]{2,1,0:T(8,128)(2,1)} async-done(((bf16[4,1024,1024]{2,1,0:T(8,128)(2,1)}), bf16[4,128,1024]{2,1,0:T(8,128)(2,1)}) %reduce-scatter.3.cloned.1.call-update) | async-done | bytes 1048592 | tf_op jit(solution)/shard_map/reduce_scatter | solution.py:19
  1527.0 2.3 slice_convert_fusion.2
  1529.3 1.1 bitcast_convert_fusion
  1530.4 1.6 copy.99
  1532.0 2.9 copy.97
  1534.9 1.2 slice.102
  1536.1 1.2 multiply_subtract_fusion.1
  1537.3 1.3 pad_maximum_fusion.3
  1541.4 6.4 fusion.47
  1547.8 34.2 %pad_maximum_fusion = f32[1024,12288]{1,0:T(8,128)} fusion(f32[1024,4096]{1,0:T(8,128)} %copy.110, f32[1024,1024]{1,0:T(8,128)} %fusion.38, f32[1024,4096]{1,0:T(8,128)} %fusion.34, f32[1024,3072]{1,0:T(8,128)} %fusion.47), kind=kLoop, calls=%fused_computation | loop fusion | flops 37748736 | bytes 100663296 | tf_op jit(solution)/shard_map/concatenate | solution.py:66
  1582.0 1.0 copy-done.12
  1583.2 5.9 fusion.23
  1589.1 1.6 fusion.30
  1591.6 4.8 fusion.49
  1596.5 2.8 fusion.51
  1599.4 74.4 %all-reduce.7 = (f32[1024]{0:T(1024)S(1)}, f32[1024]{0:T(1024)S(1)}, f32[1024]{0:T(1024)S(1)}, f32[1024]{0:T(1024)S(1)}, f32[3072]{0:T(1024)S(1)}, /*index=5*/f32[1024]{0:T(1024)S(1)}, f32[4096]{0:T(1024)S(1)}) all-reduce(f32[1024]{0:T(1024)S(1)} %get-tuple-element.82, ...), channel_id=3, replica_groups=mesh['dp'=16,'ctx'=8] {'dp','ctx'}, use_global_device_ids=true, to_apply=%region_9.10.clone | all-reduce | flops 12288 | bytes 98304
  1677.3 1.2 add_convert_fusion
  1678.5 673.0 %reduce-scatter.5.cloned.1.call-done = f32[8,12288]{1,0:T(8,128)} async-done(((f32[1024,12288]{1,0:T(8,128)}), f32[8,12288]{1,0:T(8,128)}) %reduce-scatter.5.cloned.1.call-update) | async-done | bytes 393232 | tf_op jit(solution)/shard_map/reduce_scatter | solution.py:253
  2351.6 1.6 fusion.60
  2353.9 1.5 slice.104
  2355.5 1.4 slice.105
  (135 shorter events, 21.5 us)
Async XLA Ops:
  7.2 315.7 %all-gather.7.cloned.1.call-start = ((), (), s32[]{:S(2)}) async-start(), calls=%async_computation.2 | async-start | bytes 6340608 | tf_op jit(solution)/shard_map/all_gather | solution.py:102
  7.9 618.6 %all-gather.13.cloned.1.call-start = ((), (), s32[]{:S(2)}) async-start(), calls=%async_computation.5 | async-start | bytes 2113536 | tf_op jit(solution)/shard_map/all_gather | solution.py:142
  8.7 699.7 %all-gather.11.cloned.1.call-start = ((), (), s32[]{:S(2)}) async-start(), calls=%async_computation.4 | async-start | bytes 4718592 | tf_op jit(solution)/shard_map/all_gather | solution.py:118
  11.2 316.2 %copy-start.30 = (f32[256]{0:T(256)}, f32[256]{0:T(256)S(1)}, u32[]{:S(2)}) copy-start(f32[256]{0:T(256)S(1)} %get-tuple-element.107) | copy-start | bytes 3076
  12.5 314.9 %copy-start.32 = (f32[256]{0:T(256)}, f32[256]{0:T(256)S(1)}, u32[]{:S(2)}) copy-start(f32[256]{0:T(256)S(1)} %rsqrt_bitcast_fusion) | copy-start | bytes 3076
  13.3 326.6 %copy-start.25 = (f32[2,128,8]{1,2,0:T(8,128)}, f32[2,128,8]{1,2,0:T(8,128)S(1)}, u32[]{:S(2)}) copy-start(f32[2,128,8]{1,2,0:T(8,128)S(1)} %get-tuple-element.106) | copy-start | bytes 24580
  15.5 311.9 %copy-start.17 = (bf16[256,1024]{1,0:T(8,128)(2,1)}, bf16[256,1024]{1,0:T(8,128)(2,1)S(1)}, u32[]{:S(2)}) copy-start(bf16[256,1024]{1,0:T(8,128)(2,1)S(1)} %get-tuple-element.92) | copy-start | bytes 1572868
  327.5 1.6 copy-start.20
  330.0 1.0 copy-start.16
  336.5 290.0 %copy-start.11 = (bf16[2,128,1024]{2,1,0:T(8,128)(2,1)S(1)}, bf16[2,128,1024]{2,1,0:T(8,128)(2,1)}, u32[]{:S(2)}) copy-start(bf16[2,128,1024]{2,1,0:T(8,128)(2,1)} %param.29) | copy-start | bytes 1572868
  342.4 439.1 %all-gather.9.cloned.1.call-start = ((), (), s32[]{:S(2)}) async-start(), calls=%async_computation.3 | async-start | bytes 4718592 | tf_op jit(solution)/shard_map/all_gather | solution.py:119
  344.5 748.7 %all-gather.17.cloned.1.call-start = ((), (), s32[]{:S(2)}) async-start(), calls=%async_computation.7 | async-start | bytes 8454144 | tf_op jit(solution)/shard_map/all_gather | solution.py:143
  346.1 1061.2 %all-gather.15.cloned.1.call-start = ((), (), s32[]{:S(2)}) async-start(), calls=%async_computation.6 | async-start | bytes 8454144 | tf_op jit(solution)/shard_map/all_gather | solution.py:103
  346.7 1180.3 %reduce-scatter.3.cloned.1.call-start = ((), (), s32[]{:S(2)}) async-start(), calls=%async_computation.8 | async-start | bytes 9437184 | tf_op jit(solution)/shard_map/reduce_scatter | solution.py:19
  628.9 79.5 %copy-start.23 = (bf16[2,128,16,8]{1,3,2,0:T(8,128)(2,1)S(1)}, bf16[2,128,16,8]{1,3,2,0:T(8,128)(2,1)}, u32[]{:S(2)}) copy-start(bf16[2,128,16,8]{1,3,2,0:T(8,128)(2,1)} %get-tuple-element.96) | copy-start | bytes 196612
  628.9 79.4 %copy-start.24 = (bf16[2,128,16,8]{1,3,2,0:T(8,128)(2,1)S(1)}, bf16[2,128,16,8]{1,3,2,0:T(8,128)(2,1)}, u32[]{:S(2)}) copy-start(bf16[2,128,16,8]{1,3,2,0:T(8,128)(2,1)} %get-tuple-element.97) | copy-start | bytes 196612
  713.7 5.8 copy-start
  811.8 4.5 copy-start.1
  830.1 1521.4 %reduce-scatter.5.cloned.1.call-start = ((), (), s32[]{:S(2)}) async-start(), calls=%async_computation.9 | async-start | bytes 50724864 | tf_op jit(solution)/shard_map/reduce_scatter | solution.py:253
  1101.0 306.3 %copy-start.19 = (bf16[256,1024]{1,0:T(8,128)(2,1)S(1)}, bf16[256,1024]{1,0:T(8,128)(2,1)}, u32[]{:S(2)}) copy-start(bf16[256,1024]{1,0:T(8,128)(2,1)} %get-tuple-element.93) | copy-start | bytes 1572868
  1101.0 306.3 %copy-start.36 = (f32[4096]{0:T(1024)S(1)}, f32[4096]{0:T(1024)}, u32[]{:S(2)}) copy-start(f32[4096]{0:T(1024)} %param.26) | copy-start | bytes 49156
  1450.2 10.1 copy-start.3
  1450.2 19.2 slice-start
  1460.3 9.1 slice-start.1
  1460.3 9.1 copy-start.2
  1469.4 4.9 copy-start.13
  1472.4 1.0 copy-start.15
  1529.3 6.8 copy-start.26
  1529.3 6.9 copy-start.27
  1532.0 8.5 copy-start.5
  1538.6 2.8 copy-start.18
  1539.5 1.0 copy-start.7
  1540.4 1.0 copy-start.9
  1582.0 1.0 copy-start.12
  1583.1 5.9 copy-start.4
  1583.2 5.9 copy-start.14
  1583.2 5.9 copy-start.21
  1583.2 5.9 copy-start.28
  1583.2 5.9 copy-start.29
  1589.1 1.7 copy-start.6
  1589.1 1.7 copy-start.8
  1589.1 2.0 copy-start.10
  1589.1 7.3 slice-start.2
  1591.5 4.9 copy-start.22
  1591.5 4.9 copy-start.31
  1591.6 4.9 copy-start.33
  1591.6 4.9 copy-start.34
  1591.6 4.9 copy-start.35
  1591.6 4.9 slice-start.3
  1676.1 681.2 %copy-start.37 = (f32[8]{0:T(128)}, f32[8]{0:T(128)S(1)}, u32[]{:S(2)}) copy-start(f32[8]{0:T(128)S(1)} %dynamic-slice.5) | copy-start | bytes 100
Sparse Core Ops, SparseCore 0:
  9.7 313.0 all-gather.6
  324.5 301.9 all-gather.12
  628.7 79.5 all-gather.10
  711.1 70.3 all-gather.8
  783.6 309.6 all-gather.16
  1094.8 312.4 all-gather.14
  1411.1 115.7 reduce-scatter.2
  1582.2 769.3 reduce-scatter.4
where the time goes:
time: 2370 us; the launch traced here: 2360 us
  waiting for transfers between devices  1990 us (84%)
  matrix products  116 us (5%)
  local copies, waits for them, and re-layouts  90.4 us (4%)
  other arithmetic  74.9 us (3%)
  blocking collectives  74.4 us (3%)
    reduce_scatter x1, waiting for transfers between devices, shards(): lax.psum_scatter(make_terms(entry[3], lax.axis_size(('dp', 'ctx')) * own_...  673 us
    all_gather x1, waiting for transfers between devices, process(): lax.all_gather(project_weight, ('dp', 'ctx'), axis=0, tiled=True)  307 us
    all_gather x1, waiting for transfers between devices, process(): lax.all_gather(expand_weight, ('dp', 'ctx'), axis=0, tiled=True)  300 us
    all_gather x1, waiting for transfers between devices, process(): lax.all_gather(output_weight, ('dp', 'ctx'), axis=0, tiled=True)  279 us
    all_gather x1, waiting for transfers between devices, process(): lax.all_gather(reduce_weight, ('dp', 'ctx'), axis=0, tiled=True)  263 us
    unnamed x1, blocking collectives  74.4 us
    all_gather x1, waiting for transfers between devices, process(): lax.all_gather(keys_local.reshape(batch, local_len, D), 'ctx', axis=1, ti...  72.5 us
    reduce_scatter x1, waiting for transfers between devices, side_by_side(): lax.psum_scatter(both, axis, scatter_dimension=dim, tiled=True)  49.9 us
  transfers between devices with their start and end apart: 8, of which 8 were waited for; matrix products, arithmetic and copies ran while one was open for 9% of the time, Pallas kernels for 0%

commit v1 on v0

v1 whole, which is shorter than its diff:
```python
import jax
import jax.numpy as jnp
import numpy as np
from jax import lax
from jax.experimental import pallas as pl
from jax.experimental.pallas import tpu as pltpu
from jax.sharding import PartitionSpec as P

D = 1024
HD = 64
ROT = 16
FF = 4096
GROUPS = 4
EPSILON = 1e-05

RING = 4
TP = 8
SEQ = 4
PART = 128
HALF = RING * PART
FULL = 2 * HALF
OWN = 8
LANES = 128
QKV = 3 * LANES
HID = GROUPS * LANES
WIDE = QKV + HID
SCALE = HD ** (-0.5)
BLOCK = 256

MESH = pl.DeviceIdType.MESH
VMEM = pl.BlockSpec(memory_space=pltpu.VMEM)
BF = jnp.bfloat16
F32 = jnp.float32


def place():
    dp, ctx = lax.axis_index("dp"), lax.axis_index("ctx")
    return ctx % 4, (ctx // 4) * 2 + dp // 8, (dp // 2) % 4, dp % 2


def device(x, y, z, core):
    return {"dp": ((y % 2) * 4 + z) * 2 + core, "ctx": (y // 2) * 4 + x}


class Wire:
    def __init__(self, send, recv):
        self.send, self.recv, self.copies = send, recv, []

    def push(self, src, dst, to):
        i = len(self.copies)
        copy = pltpu.make_async_remote_copy(
            src_ref=src,
            dst_ref=dst,
            send_sem=self.send.at[i],
            recv_sem=self.recv.at[i],
            device_id=to,
            device_id_type=MESH,
        )
        copy.start()
        self.copies.append(copy)
        return copy


def greet(senders, count):
    barrier = pltpu.get_barrier_semaphore()
    for other in senders:
        pl.semaphore_signal(barrier, inc=1, device_id=other, device_id_type=MESH)
    pl.semaphore_wait(barrier, count)


def row_owner(x, y, z, core):
    ylo = y % 2
    return device(ylo * 2 + z // 2, core * 2 + y // 2, (x + 3 + 2 * ylo) % 4, z % 2)


def row_source(x, y, z, core):
    ylo = x // 2
    return device((z + 1 + 2 * ylo) % 4, (y % 2) * 2 + ylo, (x % 2) * 2 + core, y // 2)


def row_block(x, y, z):
    return y, (z + 1 + 2 * (x // 2)) % 4


def fold(rows):
    return jnp.concatenate([rows[:, : D // 2], rows[:, D // 2 :]], axis=0).astype(BF)


def unfold(rows):
    return jnp.concatenate([rows[:OWN], rows[OWN:]], axis=1)


def mul(a, b, ca=1, cb=0):
    return lax.dot_general(a, b, (((ca,), (cb,)), ((), ())), preferred_element_type=F32)


def lane_of(rows):
    return lax.broadcasted_iota(jnp.int32, (rows, LANES), 1)


def turn(v, cosine, sine):
    low = lane_of(v.shape[0]) % HD < ROT // 2
    mate = jnp.where(low, pltpu.roll(v, LANES - ROT // 2, 1), pltpu.roll(v, ROT // 2, 1))
    return v * cosine + mate * sine


def column(row):
    r = lax.broadcasted_iota(jnp.int32, (PART, PART), 0)
    c = lax.broadcasted_iota(jnp.int32, (PART, PART), 1)
    return jnp.sum(jnp.where(r == c, row, 0.0), axis=1, keepdims=True)


def colsum(v):
    return jnp.sum(v, axis=0, keepdims=True)


SCRATCH = dict(
    pe_s=((TP, OWN, WIDE), F32),
    stage=((2, 4, OWN, WIDE), F32),
    wpe=((2, 4, 2, 2, 4 * OWN, WIDE), BF),
    wo_own=((2 * OWN, D // 2), BF),
    wr_f=((GROUPS, OWN, D), F32),
    wr_own=((GROUPS * OWN, D), BF),
    wos=((4, 4, 2 * OWN, D // 2), BF),
    wrs=((4, 4, GROUPS * OWN, D), BF),
    wo=((LANES, D), BF),
    wr=((HID, D), BF),
    xs=((SEQ, RING, PART, D), BF),
    gs=((SEQ, RING, PART, D), BF),
    ps=((2, 8, FULL), F32),
    first=((SEQ, RING, PART, D), BF),
    second=((SEQ, RING, PART, D), BF),
    tab=((SEQ, RING, PART, LANES), F32),
    qs=((SEQ, RING, PART, LANES), BF),
    kv=((2, SEQ, 2, RING, PART, LANES), BF),
    att=((SEQ, HALF, LANES), BF),
    hid=((SEQ, RING, PART, HID), BF),
    dexp=((SEQ, RING, PART, HID), BF),
    datt=((SEQ, RING, PART, LANES), BF),
    dkv_own=((SEQ, 2, LANES, HALF), F32),
    dkv_out=((SEQ, 2, LANES, HALF), BF),
    dkv_in=((SEQ, 2, LANES, HALF), BF),
    dproj=((SEQ, HALF, QKV), BF),
    ob=((2, 2, RING, PART, D), BF),
    half=((2, RING, PART, D), BF),
    ring_o=((2, 3, PART, D), BF),
    ring_h=((2, 3, PART, D), BF),
    small=((8, D), F32),
    small_in=((6, 8, D), F32),
    small_b=((8, D), F32),
    small_g=((8, D), F32),
    small_all=((TP, 8, D), F32),
    rg_z=((3, 4, GROUPS * OWN, D), BF),
    rg_b=((4, GROUPS * OWN, D), BF),
    rg_y=((3, GROUPS * OWN, D), BF),
    rg_f=((GROUPS * OWN, D), F32),
    rg_all=((GROUPS * OWN, D), F32),
    og_z=((3, 4, 2 * OWN, D // 2), BF),
    og_b=((4, 2 * OWN, D // 2), BF),
    og_y=((3, 2 * OWN, D // 2), BF),
    og_f=((OWN, D), F32),
    eg=((2, 4, 2, 2, 4 * OWN, HID), BF),
    eg_z=((3, 2, 2, 2, 4 * OWN, HID), BF),
    eg_b=((2, 2, 2, 4 * OWN, HID), BF),
    eg_y=((3, 2, 4 * OWN, HID), BF),
    eg_f=((2, 4, OWN, HID), F32),
    eg_all=((TP, OWN, HID), F32),
    pg=((2, 4, 2, 2, 4 * OWN, QKV), BF),
    pg_z=((3, 2, 2, 2, 4 * OWN, QKV), BF),
    pg_b=((2, 2, 2, 4 * OWN, QKV), BF),
    pg_y=((3, 2, 4 * OWN, QKV), BF),
    pg_f=((2, 4, OWN, QKV), F32),
    pg_all=((TP, OWN, QKV), F32),
)
COPIES = 176


def block_kernel(
    x_ref, g_ref, pos_ref, inv_ref, g1, s1, g2, s2, pw_ref, bp_ref, ow_ref, bo_ref, ew_ref, be_ref,
    rw_ref, br_ref,
    out_ref, dx_ref, pwg_ref, owg_ref, ewg_ref, rwg_ref, whole_ref, table_ref,
    *scratch,
):
    b = dict(zip(SCRATCH, scratch))
    send, recv = scratch[len(SCRATCH) :]
    xs, gs, ps, first, second, tab = (b[n] for n in ("xs", "gs", "ps", "first", "second", "tab"))
    wpe, wos, wrs, wo, wr, kv = (b[n] for n in ("wpe", "wos", "wrs", "wo", "wr", "kv"))
    small = b["small"]
    x, y, z, core = place()
    me = (x, y, z, core)
    t = x * 2 + core
    ylo, yhi = y % 2, y // 2
    sib = device(x, y, z, 1 - core)
    xp = [device((x + d) % 4, y, z, core) for d in (1, 2, 3)]
    xq = [device((x + d) % 4, y, z, 1 - core) for d in (1, 2, 3)]
    yp = [device(x, (y + d) % 4, z, core) for d in (1, 2, 3)]
    zp = [device(x, y, (z + d) % 4, core) for d in (1, 2, 3)]
    mine = pl.ds(2 * core, 2)
    group = [(x, 1 - core, sib)]
    group += [((x + d) % 4, core, xp[d - 1]) for d in (1, 2, 3)]
    group += [((x + d) % 4, 1 - core, xq[d - 1]) for d in (1, 2, 3)]
    t128 = pl.multiple_of(t * LANES, LANES)

    pw, ew = pw_ref[...].astype(F32), ew_ref[...].astype(F32)
    for u in range(TP):
        for m in range(3):
            b["pe_s"][u, :, m * LANES : (m + 1) * LANES] = pw[:, m * D + u * LANES : m * D + (u + 1) * LANES]
        for k in range(GROUPS):
            at = QKV + k * LANES
            b["pe_s"][u, :, at : at + LANES] = ew[:, k * D + u * LANES : k * D + (u + 1) * LANES]
    b["wo_own"][...] = fold(ow_ref[...].astype(F32))
    for i in range(OWN):
        b["wr_f"][:, i, :] = rw_ref[i].astype(F32)
    b["wr_own"][...] = b["wr_f"][...].reshape(GROUPS * OWN, D).astype(BF)
    xs[mine, x] = x_ref[...]
    gs[mine, x] = g_ref[...]
    ps[...] = jnp.zeros_like(ps)
    ps[core, 0:2] = pos_ref[...].astype(F32)
    small[...] = jnp.zeros_like(small)
    tab[...] = jnp.zeros_like(tab)

    senders = xp + [sib] + xq + yp + zp + [row_source(*me), row_owner(*me)]
    greet(senders, len(senders))
    wire = Wire(send, recv)
    push = wire.push

    step = [push(b["pe_s"].at[ux * 2 + uc], b["stage"].at[core, x], other) for ux, uc, other in group]
    by, bz = row_block(*me[:3])
    owner = row_owner(*me)
    oy, oz = core * 2 + yhi, x
    step_rows = [
        push(b["wo_own"], wos.at[oy, oz], owner),
        push(b["wr_own"], wrs.at[oy, oz], owner),
    ]
    sp = push(ps.at[core], ps.at[core], sib)
    own = xs.at[mine, x]
    xc = [push(own, own, xp[0]), push(own, own, xp[2]), push(own, own, sib)]
    b["stage"][core, x] = b["pe_s"][t]

    def keep_turn(s, j, v, turning):
        tab[s, j] = jnp.where((lane_of(PART) % HD < ROT) == turning, v, tab[s, j])

    def angles(v):
        lane, back = lane_of(v.shape[0]), pltpu.roll(v, HD, 1)
        turned = lane % HD < ROT
        cosine = jnp.where(turned, jnp.where(lane < HD, v, back), 1.0)
        return cosine, jnp.where(turned, jnp.where(lane < HD, back, v), 0.0)

    def layer_norm(s0, count, j):
        @pl.loop(0, count)
        def _(i):
            s = s0 + i
            v = xs[s, j].astype(F32)
            mean = jnp.mean(v, axis=1, keepdims=True)
            c = v - mean
            r = lax.rsqrt(jnp.mean(c * c, axis=1, keepdims=True) + EPSILON)
            n = c * r
            first[s, j] = (n * g1[...] + s1[...]).astype(BF)
            second[s, j] = (n * g2[...] + s2[...]).astype(BF)
            keep_turn(s, j, jnp.where(lane_of(PART) < HD, mean, r), False)

    def tables(s):
        @pl.loop(0, RING)
        def _(j):
            row = ps[s // 2, s % 2 : s % 2 + 1, pl.ds(pl.multiple_of(yhi * HALF + j * PART, PART), PART)]
            angle = column(row) * inv_ref[...]
            lane = lane_of(PART)
            sign = jnp.where(lane % HD < ROT // 2, -1.0, 1.0)
            keep_turn(s, j, jnp.where(lane < HD, jnp.cos(angle), jnp.sin(angle) * sign), True)

    bias_p = jnp.concatenate([bp_ref[:, pl.ds(pl.multiple_of(m * D + t128, LANES), LANES)] for m in range(3)], axis=1)
    bias_e = jnp.concatenate(
        [be_ref[:, pl.ds(pl.multiple_of(k * D + t128, LANES), LANES)] for k in range(GROUPS)], axis=1
    )

    def project(j):
        p = mul(first[:, j].reshape(HALF, D), wpe[:, :, :, :, :, 0:QKV].reshape(D, QKV)) + bias_p
        c, s = angles(tab[:, j].reshape(HALF, LANES))
        shape = (SEQ, PART, LANES)
        b["qs"][:, j] = turn(p[:, :LANES], c, s).astype(BF).reshape(shape)
        kv[0, :, 0, j] = turn(p[:, LANES : 2 * LANES], c, s).astype(BF).reshape(shape)
        kv[1, :, 0, j] = p[:, 2 * LANES :].astype(BF).reshape(shape)
        return push(kv.at[:, :, 0, j], kv.at[:, :, 1, j], yp[1])

    def expand(j):
        e = mul(second[:, j].reshape(HALF, D), wpe[:, :, :, :, :, QKV:].reshape(D, HID)) + bias_e
        cdf = 0.5 * (1.0 + lax.erf(e * 0.5**0.5))
        b["hid"][:, j] = (e * cdf).astype(BF).reshape(SEQ, PART, HID)
        slope = cdf + e * (jnp.exp(-0.5 * e * e) * (2.0 * np.pi) ** -0.5)
        b["dexp"][:, j] = slope.astype(BF).reshape(SEQ, PART, HID)

    layer_norm(2 * core, 2, x)
    for c in step:
        c.wait_recv()
    wpe[ylo, z, :, yhi] = b["stage"][...].reshape(2, 4 * OWN, WIDE).astype(BF)
    for c in step_rows:
        c.wait_recv()
    top, low = pl.ds(0, 2 * OWN), pl.ds(2 * OWN, 2 * OWN)
    stage1 = []
    for d in (0, 2, 1):
        v = wpe.at[ylo, z, 0, yhi]
        stage1.append(push(v, v, yp[d]))
        v = wpe.at[ylo, z, 1, yhi]
        stage1.append(push(v, v, zp[d]))
    rows1 = []
    for d in (0, 2, 1):
        v = wrs.at[by, bz, top]
        rows1.append(push(v, v, yp[d]))
        v = wrs.at[by, bz, low]
        rows1.append(push(v, v, zp[d]))
        v = wos.at[by, bz]
        rows1.append(push(v, v, yp[d]))
    sp.wait_recv()
    for s in range(SEQ):
        tables(s)
    xc[2].wait_recv()
    layer_norm(2 - 2 * core, 2, x)
    for c in stage1:
        c.wait_recv()
    stage2 = []
    for d in (0, 2, 1):
        v = wpe.at[:, z, 0]
        stage2.append(push(v, v, zp[d]))
        v = wpe.at[ylo, :, 1, yhi]
        stage2.append(push(v, v, yp[d]))
    for c in rows1:
        c.wait_recv()
    rows2 = []
    for d in (0, 2, 1):
        v = wrs.at[:, bz, top]
        rows2.append(push(v, v, zp[d]))
        v = wrs.at[by, :, low]
        rows2.append(push(v, v, yp[d]))
        v = wos.at[:, bz]
        rows2.append(push(v, v, zp[d]))
    before, after, far = (x + 3) % 4, (x + 1) % 4, (x + 2) % 4

    def relay(buf, near):
        near[0].wait_recv()
        v = buf.at[2 * core, before]
        ahead = push(v, v, xp[0])
        near[1].wait_recv()
        v = buf.at[2 * core + 1, after]
        back = push(v, v, xp[2])
        v, w = buf.at[mine, before], buf.at[mine, after]
        return [ahead, back], [push(v, v, sib), push(w, w, sib)]

    def relay_far(buf, fars):
        fars[0].wait_recv()
        v = buf.at[2 * core, far]
        a = push(v, v, sib)
        fars[1].wait_recv()
        w = buf.at[2 * core + 1, far]
        return [a, push(w, w, sib)]

    xf, xd = relay(xs, xc)
    own = gs.at[mine, x]
    gc = [push(own, own, xp[0]), push(own, own, xp[2]), push(own, own, sib)]
    layer_norm(2 * core, 2, before)
    layer_norm(2 * core, 2, after)
    for c in xd:
        c.wait_recv()
    layer_norm(2 - 2 * core, 2, before)
    layer_norm(2 - 2 * core, 2, after)
    for c in stage2:
        c.wait_recv()
    kc = [project(x), project(before), project(after)]
    xfd = relay_far(xs, xf)
    expand(x)
    layer_norm(2 * core, 2, far)
    for c in xfd:
        c.wait_recv()
    layer_norm(2 - 2 * core, 2, far)
    kc.append(project(far))
    expand(before)
    gf, gd = relay(gs, gc)
    expand(after)
    expand(far)

    for c in rows2:
        c.wait_recv()
    for j in range(16):
        wo_f = unfold(wos[j // 4, j % 4].astype(F32))
        b["wr_f"][0] = wo_f
        if j % 2 == 0:
            last = wo_f
        else:
            wo[(j - 1) * OWN : (j + 1) * OWN] = jnp.concatenate([last, wo_f], axis=0).astype(BF)
    wr_all = wrs[...].reshape(16, GROUPS, OWN, D).astype(F32)
    for k in range(GROUPS):
        wr[k * LANES : (k + 1) * LANES] = wr_all[:, k].reshape(LANES, D).astype(BF)

    small[4:5] = colsum(g_ref[...].astype(F32).reshape(2 * PART, D))

    def upstream(j):
        g = gs[:, j].reshape(HALF, D)
        b["datt"][:, j] = mul(g, wo[...], 1, 1).astype(BF).reshape(SEQ, PART, LANES)
        d = mul(g, wr[...], 1, 1) * b["dexp"][:, j].reshape(HALF, HID).astype(F32)
        small[5:6, QKV:WIDE] += colsum(d)
        b["dexp"][:, j] = d.astype(BF).reshape(SEQ, PART, HID)

    gc[2].wait_recv()
    for c in gd:
        c.wait_recv()
    gfd = relay_far(gs, gf)
    upstream(x)
    upstream(before)
    upstream(after)
    for c in gfd:
        c.wait_recv()
    upstream(far)
    settled = xc + xf + xd + xfd + step_rows + rows1 + rows2
    for c in settled:
        c.wait_send()
    for c in kc:
        c.wait_recv()

    def attend(s):
        k, v = kv[0, s].reshape(FULL, LANES), kv[1, s].reshape(FULL, LANES)
        row = ps[s // 2, pl.ds(s % 2, 1), pl.ds(pl.multiple_of(yhi * HALF, HALF), HALF)]
        other = ps[s // 2, pl.ds(s % 2, 1), pl.ds(pl.multiple_of((1 - yhi) * HALF, HALF), HALF)]
        keys_at = jnp.concatenate([row, other], axis=1)
        lane = lane_of(BLOCK)
        zero = jnp.zeros((BLOCK, LANES), BF)
        dk = dv = None
        for i in range(HALF // BLOCK):
            few = slice(i * BLOCK // PART, (i + 1) * BLOCK // PART)
            at_rows = slice(i * BLOCK, (i + 1) * BLOCK)
            q, do = b["qs"][s, few].reshape(BLOCK, LANES), b["datt"][s, few].reshape(BLOCK, LANES)
            at = jnp.concatenate(
                [column(row[:, j * PART : (j + 1) * PART]) for j in range(few.start, few.stop)], axis=0
            )
            allowed = keys_at <= at
            out = jnp.zeros((BLOCK, LANES), F32)
            dq = jnp.zeros((BLOCK, LANES), F32)
            for h in range(2):
                m = lane // HD == h
                qh, doh = jnp.where(m, q, zero), jnp.where(m, do, zero)
                score = jnp.where(allowed, mul(qh, k, 1, 1) * SCALE, -1e30)
                raised = jnp.exp(score - jnp.max(score, axis=1, keepdims=True))
                p = raised * (1.0 / jnp.sum(raised, axis=1, keepdims=True))
                p_low = p.astype(BF)
                oh = jnp.where(m, mul(p_low, v), 0.0)
                out = out + oh
                delta = jnp.sum(doh.astype(F32) * oh, axis=1, keepdims=True)
                ds = (p * (mul(doh, v, 1, 1) - delta)).astype(BF)
                dq = jnp.where(m, mul(ds, k), dq)
                dkh, dvh = mul(qh, ds, 0, 0), mul(doh, p_low, 0, 0)
                dk, dv = (dkh, dvh) if dk is None else (dk + dkh, dv + dvh)
            b["att"][s, at_rows] = out.astype(BF)
            cosine, sine = angles(tab[s, few].reshape(BLOCK, LANES))
            dq = turn(dq * SCALE, cosine, -sine)
            small[5:6, :LANES] += colsum(dq)
            b["dproj"][s, at_rows, :LANES] = dq.astype(BF)
        for n, v in enumerate((dk * SCALE, dv)):
            b["dkv_own"][s, n] = v[:, :HALF]
            b["dkv_out"][s, n] = v[:, HALF:].astype(BF)

    def branches(p, c):
        s = 2 * c + p
        v = mul(b["att"][s], wo[...]) + mul(b["hid"][s].reshape(HALF, HID), wr[...])
        b["ob"][p, c] = v.astype(BF).reshape(RING, PART, D)

    def combine(ref, at, half, p):
        @pl.loop(0, RING)
        def _(i):
            ref[(*at, i)] = (ref[(*at, i)].astype(F32) + half[p, i].astype(F32)).astype(BF)

    def spread(ref, at, ring, p):
        return [push(ref.at[(*at, (x + d) % 4)], ring.at[p, d - 1], xp[d - 1]) for d in (1, 3, 2)]

    dc, oc, oring = [], [], []
    for p in range(2):

        @pl.loop(0, 2)
        def _(c):
            attend(2 * c + p)

        dc.append([push(b["dkv_out"].at[s], b["dkv_in"].at[s], yp[1]) for s in (p, 2 + p)])

        if p == 1:
            oc[0].wait_recv()
            combine(b["ob"], (0, core), b["half"], 0)
            oring.append(spread(b["ob"], (0, core), b["ring_o"], 0))

        @pl.loop(0, 2)
        def _(c):
            branches(p, c)

        oc.append(push(b["ob"].at[p, 1 - core], b["half"].at[p], sib))

    rows = SEQ * HALF
    for k in range(2):
        two = slice(2 * k * LANES, 2 * (k + 1) * LANES)
        r = mul(b["hid"][..., two].reshape(rows, 2 * LANES), gs[...].reshape(rows, D), 0, 0).reshape(2, 16, OWN, D)
        for j in range(16):
            wrs[j // 4, j % 4, 2 * k * OWN : 2 * (k + 1) * OWN] = r[:, j].reshape(2 * OWN, D).astype(BF)
    o = mul(b["att"][...].reshape(rows, LANES), gs[...].reshape(rows, D), 0, 0)
    for j in range(16):
        wos[j // 4, j % 4] = fold(o[j * OWN : (j + 1) * OWN])
    rz = []
    for d in (1, 3, 2):
        ob = (bz + d) % 4
        rz.append(push(wrs.at[:, ob], b["rg_z"].at[d - 1], zp[d - 1]))
        rz.append(push(wos.at[:, ob], b["og_z"].at[d - 1], zp[d - 1]))
    oc[1].wait_recv()
    combine(b["ob"], (1, core), b["half"], 1)
    oring.append(spread(b["ob"], (1, core), b["ring_o"], 1))

    def inward(s):
        for n in range(2):
            v = (b["dkv_own"][s, n] + b["dkv_in"][s, n].astype(F32)).T
            if n == 0:
                cosine, sine = angles(tab[s].reshape(HALF, LANES))
                v = turn(v, cosine, -sine)
            small[5:6, (n + 1) * LANES : (n + 2) * LANES] += colsum(v)
            b["dproj"][s, :, (n + 1) * LANES : (n + 2) * LANES] = v.astype(BF)

        @pl.loop(0, 2)
        def _(i):
            two = pl.ds(2 * i, 2)
            rows = 2 * PART
            da = mul(
                b["dproj"][s, pl.ds(pl.multiple_of(i * rows, rows), rows)],
                wpe[:, :, :, :, :, 0:QKV].reshape(D, QKV), 1, 1,
            )
            db = mul(
                b["dexp"][s, two].reshape(rows, HID), wpe[:, :, :, :, :, QKV:].reshape(D, HID), 1, 1
            )
            st = tab[s, two].reshape(rows, LANES)
            n = (xs[s, two].reshape(rows, D).astype(F32) - st[:, ROT : ROT + 1]) * st[:, HD + ROT : HD + ROT + 1]
            small[0:1] += colsum(da * n)
            small[1:2] += colsum(da)
            small[2:3] += colsum(db * n)
            small[3:4] += colsum(db)
            xs[s, two] = (da * g1[...] + db * g2[...]).astype(BF).reshape(2, PART, D)

    def weight_grad(into, back_ref, to):
        for i in range(4):
            v = into[..., i * 2 * LANES : (i + 1) * 2 * LANES].reshape(rows, 2 * LANES)
            back = back_ref[...].reshape(rows, back_ref.shape[-1])
            e = mul(v, back, 0, 0).astype(BF).reshape(2, 2, 2, 4 * OWN, back.shape[1])
            to[i // 2, 2 * (i % 2) : 2 * (i % 2) + 2] = e

    hc, hring = [], []
    for p in range(2):
        for c in dc[p]:
            c.wait_recv()

        @pl.loop(0, 2)
        def _(c):
            inward(2 * c + p)

        hc.append(push(xs.at[2 * (1 - core) + p], b["half"].at[p], sib))
        if p == 0:
            weight_grad(second, b["dexp"], b["eg"])
            ez = [
                push(b["eg"].at[:, (z + d) % 4], b["eg_z"].at[d - 1], zp[d - 1]) for d in (1, 3, 2)
            ]
        hc[p].wait_recv()
        combine(xs, (2 * core + p,), b["half"], p)
        hring.append(spread(xs, (2 * core + p,), b["ring_h"], p))

    sz = [push(small, b["small_in"].at[d - 1], zp[d - 1]) for d in (1, 2, 3)]
    weight_grad(first, b["dproj"], b["pg"])
    pz = [push(b["pg"].at[:, (z + d) % 4], b["pg_z"].at[d - 1], zp[d - 1]) for d in (1, 3, 2)]

    def total(first_term, inbox):
        return (
            first_term.astype(F32) + inbox[0].astype(F32) + inbox[1].astype(F32) + inbox[2].astype(F32)
        )

    for c in rz:
        c.wait_recv()
    b["rg_b"][...] = total(wrs[:, bz], b["rg_z"]).astype(BF)
    b["og_b"][...] = total(wos[:, bz], b["og_z"]).astype(BF)
    ry = []
    for d in (1, 3, 2):
        to = (y + d) % 4
        ry.append(push(b["rg_b"].at[to], b["rg_y"].at[d - 1], yp[d - 1]))
        ry.append(push(b["og_b"].at[to], b["og_y"].at[d - 1], yp[d - 1]))

    def along_y(name, arrived):
        for c in arrived:
            c.wait_recv()
        b[name + "_b"][...] = total(b[name][:, z], b[name + "_z"]).astype(BF)
        out = []
        for d in (1, 3, 2):
            to = (y + d) % 4
            out.append(push(b[name + "_b"].at[to % 2, :, to // 2], b[name + "_y"].at[d - 1], yp[d - 1]))
        return out

    def to_owners(name, arrived):
        for c in arrived:
            c.wait_recv()
        width = b[name + "_f"].shape[-1]
        v = total(b[name + "_b"][ylo, :, yhi], b[name + "_y"])
        b[name + "_f"][...] = v.reshape(2, 4, OWN, width)
        b[name + "_all"][t] = b[name + "_f"][core, x]
        return [
            push(b[name + "_f"].at[uc, ux], b[name + "_all"].at[t], other) for ux, uc, other in group
        ]

    ey = along_y("eg", ez)
    for c in sz:
        c.wait_recv()
    b["small_b"][...] = small[...] + b["small_in"][0] + b["small_in"][1] + b["small_in"][2]
    sy = [push(b["small_b"], b["small_in"].at[2 + d], yp[d - 1]) for d in (1, 2, 3)]
    for c in ry:
        c.wait_recv()
    b["rg_f"][...] = total(b["rg_b"][y], b["rg_y"])
    b["og_f"][...] = unfold(total(b["og_b"][y], b["og_y"]))
    source = row_source(*me)
    back = [push(b["rg_f"], b["rg_all"], source), push(b["og_f"], owg_ref, source)]
    eo = to_owners("eg", ey)
    for c in sy:
        c.wait_recv()
    b["small_g"][...] = (
        b["small_b"][...] + b["small_in"][3] + b["small_in"][4] + b["small_in"][5]
    )
    b["small_all"][t] = b["small_g"][...]
    so = [push(b["small_g"], b["small_all"].at[t], other) for _, _, other in group]
    py = along_y("pg", pz)
    for p in range(2):
        for c in oring[p]:
            c.wait_recv()
        v = total(b["ob"][p, core, x], b["ring_o"].at[p])
        out_ref[p] = (x_ref[p].astype(F32) + v + bo_ref[...] + br_ref[...]).astype(BF)
    po = to_owners("pg", py)
    for c in back:
        c.wait_recv()
    r = b["rg_all"][...].reshape(GROUPS, OWN, D)
    for k in range(GROUPS):
        rwg_ref[:, k, :] = r[k]
    for c in eo:
        c.wait_recv()
    for u in range(TP):
        for k in range(GROUPS):
            ewg_ref[:, k * D + u * LANES : k * D + (u + 1) * LANES] = b["eg_all"][u, :, k * LANES : (k + 1) * LANES]
    for c in so:
        c.wait_recv()
    whole_ref[...] = sum(b["small_all"][u] for u in range(TP))
    for u in range(TP):
        for k in range(7):
            table_ref[0:1, k * D + u * LANES : k * D + (u + 1) * LANES] = b["small_all"][
                u, 5:6, k * LANES : (k + 1) * LANES
            ]
    for p in range(2):
        for c in hring[p]:
            c.wait_recv()
        h = total(xs[2 * core + p, x], b["ring_h"].at[p])
        st = tab[2 * core + p, x]
        r = st[:, HD + ROT : HD + ROT + 1]
        n = (x_ref[p].astype(F32) - st[:, ROT : ROT + 1]) * r
        inner = (
            h - jnp.mean(h, axis=1, keepdims=True) - n * jnp.mean(h * n, axis=1, keepdims=True)
        )
        dx_ref[p] = (g_ref[p].astype(F32) + r * inner).astype(BF)
    for c in po:
        c.wait_recv()
    for u in range(TP):
        for m in range(3):
            pwg_ref[:, m * D + u * LANES : m * D + (u + 1) * LANES] = b["pg_all"][u, :, m * LANES : (m + 1) * LANES]
    for c in wire.copies:
        if not any(c is w for w in settled):
            c.wait_send()


def shards(
    inputs, positions, first_gain, first_shift, second_gain, second_shift, project_weight,
    project_bias, output_weight, output_bias, expand_weight, expand_bias, reduce_weight,
    reduce_bias, cotangent,
):
    inverse = 10000.0 ** (-(np.arange(ROT // 2, dtype=np.float32) * 2.0 / ROT))
    by_lane = np.zeros((2, HD), np.float32)
    by_lane[:, :ROT] = np.concatenate([inverse, inverse]).astype(np.float32)
    line = lambda v: v.reshape(1, -1)
    shape = jax.ShapeDtypeStruct
    out, dx, pwg, owg, ewg, rwg, whole, table = pl.pallas_call(
        block_kernel,
        name="block",
        out_shape=(
            shape((2, PART, D), BF),
            shape((2, PART, D), BF),
            shape((OWN, 3 * D), F32),
            shape((OWN, D), F32),
            shape((OWN, FF), F32),
            shape((OWN, GROUPS, D), F32),
            shape((8, D), F32),
            shape((1, 7 * D), F32),
        ),
        in_specs=[VMEM] * 16,
        out_specs=(VMEM,) * 8,
        scratch_shapes=[pltpu.VMEM(*v) for v in SCRATCH.values()]
        + [pltpu.SemaphoreType.DMA((COPIES,)), pltpu.SemaphoreType.DMA((COPIES,))],
        compiler_params=pltpu.CompilerParams(
            collective_id=0, has_side_effects=True, vmem_limit_bytes=64 * 2**20
        ),
    )(
        inputs, cotangent, positions, jnp.asarray(by_lane.reshape(1, LANES)),
        line(first_gain), line(first_shift), line(second_gain), line(second_shift),
        project_weight, line(project_bias), output_weight, line(output_bias),
        expand_weight, line(expand_bias), reduce_weight, line(reduce_bias),
    )
    index = lax.axis_index("dp") * 8 + lax.axis_index("ctx")
    vec = lax.dynamic_slice_in_dim(whole, index * 8, 8, 1)
    bpg = lax.dynamic_slice_in_dim(table[0, : 3 * D], index * 24, 24, 0)
    beg = lax.dynamic_slice_in_dim(table[0, 3 * D :], index * 32, 32, 0)
    return (
        out, dx, vec[0], vec[1], vec[2], vec[3], pwg, bpg, owg, vec[4], ewg, beg, rwg, vec[4],
    )


def solution(mesh):
    rows = P(("dp", "ctx"), None)
    vector = P(("dp", "ctx"))
    tokens = P("dp", "ctx", None)
    deep = P(("dp", "ctx"), None, None)
    return jax.shard_map(
        shards,
        mesh=mesh,
        in_specs=(
            tokens, P("dp", None), P(), P(), P(), P(), rows, P(), rows, P(), rows, P(), deep, P(),
            tokens,
        ),
        out_specs=(
            tokens, tokens, vector, vector, vector, vector, rows, vector, rows, vector, rows,
            vector, deep, vector,
        ),
        check_vma=False,
    )
```

time: 2370 us -> 162 us (0.07)
  the two profiles are of different devices: /device:TPU:0 before, /device:TPU:49 now
where the time goes in v1:
time: 162 us
  Pallas kernels  152 us (94%)
  local copies, waits for them, and re-layouts  8.84 us (5%)
    pallas_call x1, Pallas kernels, shards(): pl.pallas_call(block_kernel, name='block', out_shape=(shape((2, PART, D),...  152 us
    unnamed x21, local copies, waits for them, and re-layouts  6.39 us

profile of v1, /device:TPU:49, one launch (start us, length us, event | category | flops | bytes accessed | tf_op | source)
XLA Modules:
  0.0 161.6 jit_solution(6442382545960334450)
XLA Ops:
  0.7 152.1 %block.1 = (bf16[2,128,1024]{2,1,0:T(8,128)(2,1)}, bf16[2,128,1024]{2,1,0:T(8,128)(2,1)}, f32[8,3072]{1,0:T(8,128)}, f32[8,1024]{1,0:T(8,128)}, f32[8,4096]{1,0:...) custom-call(bf16[2,128,1024]{2,1,0:T(8,128)(2,1)} %x_ref.1, bf16[2,128,1024]{2,1,0:T(8,128)(2,1)} %g_ref.1, ...), custom_call_target="tpu_custom_call" | custom-call | tf_op jit(solution)/shard_map/block/pallas_call | solution.py:679
  152.8 0.0 copy-start.5
  152.8 0.8 constant_dynamic-slice_fusion.2
  153.5 0.5 slice_bitcast_fusion
  154.1 0.0 copy-start.6
  154.1 0.0 copy-done.5
  154.1 0.6 fusion.1
  154.7 0.6 fusion
  155.3 0.0 copy-done.6
  155.3 0.5 copy.37
  155.8 0.0 copy-start
  155.8 1.9 %copy.38 = bf16[2,128,1024]{2,1,0:T(8,128)(2,1)} copy(bf16[2,128,1024]{2,1,0:T(8,128)(2,1)} %get-tuple-element.77) | data formatting | bytes 1048576
  157.7 0.0 copy-done
  157.7 0.0 copy-start.3
  157.7 0.8 copy.39
  158.5 0.2 copy-done.3
  158.7 0.0 copy-start.4
  158.7 0.0 copy-start.2
  158.7 0.6 copy.40
  159.3 0.1 copy-done.4
  159.4 0.6 copy.41
  160.0 0.0 copy-done.2
  160.0 0.0 copy-start.1
  160.0 0.7 copy.42
  160.7 0.3 copy-done.1
  161.0 0.7 copy.43
  (2 shorter events, 0.0 us)
Async XLA Ops:
  152.8 1.3 copy-start.5
  154.1 1.2 copy-start.6
  155.8 1.9 %copy-start = (bf16[2,128,1024]{2,1,0:T(8,128)(2,1)S(1)}, bf16[2,128,1024]{2,1,0:T(8,128)(2,1)}, u32[]{:S(2)}) copy-start(bf16[2,128,1024]{2,1,0:T(8,128)(2,1)} %get-tuple-element.78) | copy-start | bytes 1572868
  157.7 1.0 copy-start.3
  158.7 0.8 copy-start.4
  158.7 1.4 copy-start.2
  160.0 1.0 copy-start.1
